TPU v7x, 512 devices: a whole 4x4x16 slice. The times are simulated.
512 devices in a mesh: tm: 64 (over x, z), mp: 8 (over y, core).
Axes of the slice: x: 4, y: 4, z: 16, core: 2. Of those that a mesh axis runs over, the one named last changes fastest.
Arguments:
- observations: bfloat16 [64, 4096, 256], P('tm', None, 'mp'), may hold values from -6 to 6
- contact: int32 [512, 8, 8], P('tm'), may hold values 0 or 1
- resets: int32 [8, 4096], P(None, 'tm'), may hold values 0 or 1
- q_weight: bfloat16 [2048, 1024], P(None, 'mp'), may hold values from -0.125 to 0.125
- k_weight: bfloat16 [2048, 1024], P(None, 'mp'), may hold values from -0.125 to 0.125
- v_weight: bfloat16 [2048, 1024], P(None, 'mp'), may hold values from -0.125 to 0.125
- decay_weight: bfloat16 [2048, 1024], P(None, 'mp'), may hold values from -0.125 to 0.125
- gate_weight: bfloat16 [2048, 1024], P(None, 'mp'), may hold values from -0.125 to 0.125
- decay_bias: float32 [8, 128], P('mp'), may hold values from 4 to 14
- norm_gain: float32 [8, 128], P('mp'), may hold values from 0.25 to 1.75
- out_weight: bfloat16 [1024, 2048], P(None, 'mp'), may hold values from -0.1875 to 0.1875
- out_cotangent: bfloat16 [8, 4096, 2048], P(None, 'tm', 'mp'), may hold values from -0.03125 to 0.03125
Outputs:
- following_frame: bfloat16 [8, 4096, 2048], P(None, 'tm', 'mp')
- out_weight_grad: float32 [1024, 2048], P('tm', 'mp')
All inputs are finite; a program needn't handle non-finite values. No bound on the sum of `contact` or of `resets` on one device may be relied on, other than what follows from the above.
Results may differ from a plain program's by a relative error of at most 0.0049.
Values may be sent and summed in bfloat16 or wider, within the bound.
A program may use at most 128 MiB of HBM per device.

v0:
```python
import jax
import jax.numpy as jnp
from jax import lax
from jax.sharding import PartitionSpec as P

HK = 128
CH = 8


def prefix(part, axis, combine, identity):
    place = lax.axis_index(axis)
    gathered = jax.tree.map(lambda a: lax.all_gather(a, axis), part)
    state = jax.tree.map(lambda a, e: jnp.zeros_like(a) + jnp.asarray(e, a.dtype), part, identity)

    def one(hop, state):
        return combine(
            state, jax.tree.map(lambda a: lax.dynamic_index_in_dim(a, hop, 0, False), gathered)
        )

    return lax.fori_loop(0, place, one, state)


def block_terms(queries, key_rows, value_rows, log_decay, reset_block):
    frames = queries.shape[2]
    log_total = jnp.cumsum(log_decay, axis=2)
    resets_observed = jnp.cumsum(reset_block, axis=1)
    last_total = log_total[:, :, -1, :]
    last_seen = resets_observed[:, -1]
    untouched = (resets_observed == 0).astype(jnp.float32)[:, None, :, None]
    survives = (resets_observed == last_seen[:, None]).astype(jnp.float32)[:, None, :, None]
    block_decay = jnp.exp(last_total) * (last_seen == 0).astype(jnp.float32)[:, None, None]
    weights = jnp.exp(last_total[:, :, None, :] - log_total) * survives
    block_state = jnp.einsum(
        "chtk,chtv->chkv", key_rows * weights, value_rows, precision=lax.Precision.HIGHEST
    )
    carried_q = queries * jnp.exp(log_total) * untouched
    middle = log_total[:, :, frames // 2 : frames // 2 + 1, :]
    scaled_q = queries * jnp.exp(log_total - middle)
    scaled_k = key_rows * jnp.exp(middle - log_total)
    scores = jnp.einsum("chtk,chsk->chts", scaled_q, scaled_k, precision=lax.Precision.HIGHEST)
    row_index = lax.broadcasted_iota(jnp.int32, (frames, frames), 0)
    earlier = lax.broadcasted_iota(jnp.int32, (frames, frames), 1)
    causal = (row_index >= earlier)[None, :, :] & (
        resets_observed[:, :, None] == resets_observed[:, None, :]
    )
    scores = jnp.where(causal[:, None, :, :], scores, 0.0)
    inside = jnp.einsum("chts,chsv->chtv", scores, value_rows, precision=lax.Precision.HIGHEST)
    return (block_decay, block_state, carried_q, inside)


def finish(attended, gate_values, gain_head, links_block):
    characters, head_count, frames, value_width = attended.shape
    blocks = links_block.shape[0]
    mean_square = jnp.mean(attended * attended, axis=-1, keepdims=True)
    normed = attended * lax.rsqrt(mean_square + 1e-06) * gain_head[None, :, None, :]
    normed = normed.transpose(0, 2, 1, 3).reshape(characters, frames, head_count * value_width)
    regrouped_rows = normed.reshape(characters, blocks, frames // blocks * head_count * value_width)
    contact_factor = links_block.astype(jnp.float32)
    total_rows = jnp.einsum(
        "nmr,rnd->mnd", contact_factor, regrouped_rows, precision=lax.Precision.HIGHEST
    )
    partners = jnp.maximum(jnp.sum(contact_factor, axis=-1), 1.0)
    mixed_rows = regrouped_rows + total_rows / jnp.transpose(partners)[:, :, None]
    mixed_rows = mixed_rows.reshape(characters, frames, head_count * value_width)
    return (mixed_rows * jax.nn.silu(gate_values)).astype(jnp.bfloat16)


def combine_states(earlier, later_part):
    return (earlier[0] * later_part[0], later_part[0][..., None] * earlier[1] + later_part[1])


def local(
    observations,
    contact,
    resets,
    q_weight,
    k_weight,
    v_weight,
    decay_weight,
    gate_weight,
    decay_bias,
    norm_gain,
    out_weight,
    out_cotangent,
):
    span_time = lax.axis_size("tm")
    splits = span_time // CH
    characters = resets.shape[0]
    frames = resets.shape[1]
    head_count = decay_bias.shape[0]
    matrices = (q_weight, k_weight, v_weight, decay_weight, gate_weight)
    zero_sums = tuple(
        (jnp.zeros((characters, frames, matrix.shape[1]), jnp.float32) for matrix in matrices)
    )
    full_rows = lax.all_gather(observations, "mp", axis=2, tiled=True)
    rollout = lax.all_to_all(full_rows, "tm", split_axis=1, concat_axis=0, tiled=True)
    span_width = rollout.shape[2]
    regrouped_rows = rollout.reshape(characters, splits, frames, span_width)
    result = []
    for partial_sum, matrix in zip(zero_sums, matrices):
        blocked = matrix.reshape(splits, matrix.shape[0] // splits, matrix.shape[1])
        result.append(
            jnp.einsum("cgtf,gfh->cth", regrouped_rows, blocked, preferred_element_type=jnp.float32)
        )
    projected = tuple(result)

    def head_major(values):
        return values.reshape(characters, frames, head_count, -1).transpose(0, 2, 1, 3)

    queries = head_major(projected[0] * HK ** (-0.5))
    key_rows = head_major(projected[1])
    value_rows = head_major(projected[2])
    log_decay = head_major(
        jax.nn.log_sigmoid(projected[3].reshape(characters, frames, head_count, -1) + decay_bias)
    )
    block_decay, block_state, carried_q, inside = block_terms(
        queries, key_rows, value_rows, log_decay, resets
    )
    identity = (jnp.ones_like(block_decay), jnp.zeros_like(block_state))
    entering = prefix((block_decay, block_state), "tm", combine_states, identity)
    attended = inside + jnp.einsum(
        "chtk,chkv->chtv", carried_q, entering[1], precision=lax.Precision.HIGHEST
    )
    gated = finish(attended, projected[4], norm_gain, contact)
    gated_rows = gated.reshape(characters * frames, -1)
    cotangent_rows = out_cotangent.reshape(characters * frames, -1)
    portion = lax.all_gather(gated_rows, "mp", axis=1, tiled=True)
    produced = jnp.dot(portion, out_weight, preferred_element_type=jnp.float32)
    gradient_piece = lax.dot_general(
        portion, cotangent_rows, (((0,), (0,)), ((), ())), preferred_element_type=jnp.float32
    )
    produced, partial_grad = (produced, gradient_piece)
    following_frame = produced.astype(jnp.bfloat16).reshape(characters, frames, -1)
    weight_grad = lax.psum_scatter(partial_grad, "tm", scatter_dimension=0, tiled=True)
    return (following_frame, weight_grad)


def solution(mesh):
    placed = (
        P("tm", None, "mp"),
        P("tm", None, None),
        P(None, "tm"),
        P(None, "mp"),
        P(None, "mp"),
        P(None, "mp"),
        P(None, "mp"),
        P(None, "mp"),
        P("mp", None),
        P("mp", None),
        P(None, "mp"),
        P(None, "tm", "mp"),
    )
    return jax.shard_map(
        local,
        mesh=mesh,
        in_specs=placed,
        out_specs=(P(None, "tm", "mp"), P("tm", "mp")),
        check_vma=False,
    )
```

profile of v0, /device:TPU:8, one launch (start us, length us, event | category | flops | bytes accessed | tf_op | source)
XLA Modules:
  0.0 1353.7 jit_solution(6704598011931905069)
XLA Ops:
  7.2 0.0 copy-start
  7.2 0.0 all-gather.5.cloned.1.call-start
  7.2 0.7 all-gather.5.cloned.1.call-update
  7.9 38.6 %all-gather.5.cloned.1.call-done = bf16[1,4096,256]{1,2,0:T(8,128)(2,1)} async-done(((bf16[1,4096,32]{1,2,0:T(8,128)(2,1)}), bf16[1,4096,256]{1,2,0:T(8,128)(2,1)}) %all-gather.5.cloned.1.call-update) | async-done | bytes 2097168 | tf_op jit(solution)/shard_map/all_gather | solution.py:95
  46.5 10.0 copy.41
  56.5 0.5 broadcast.79
  57.0 21.6 %reduce.4 = bf16[4096,256]{1,0:T(8,128)(2,1)S(1)} reduce(bf16[4096,1,256]{2,1,0:T(2,128)(2,1)} %bitcast.127, bf16[]{:T(256)} %broadcast.79), dimensions={1}, to_apply=%bitcast.99.reduce_sub_computation | reduce | bytes 4194306
  78.6 2.1 reshape.229
  80.7 15.7 %all-to-all-start = ((bf16[64,2,8192]{2,1,0:T(2,128)(2,1)}), bf16[64,2,8192]{2,1,0:T(2,128)(2,1)S(1)}, u32[]{:S(2)}, u32[]{:S(2)}) async-start(bf16[64,2,8192]{2,1,0:T(2,128)(2,1)} %reshape.229), calls=%async_computation | async-start | bytes 4194304 | tf_op jit(solution)/shard_map/all_to_all | solution.py:96
  96.5 0.0 all-gather.9.cloned.1.call-start
  96.5 0.2 reduce_window_sum.24
  96.7 0.2 slice_reduce_fusion
  96.9 0.1 compare_convert_fusion.1
  97.0 97.4 %all-to-all-done = bf16[64,2,8192]{2,1,0:T(2,128)(2,1)S(1)} async-done(((bf16[64,2,8192]{2,1,0:T(2,128)(2,1)}), bf16[64,2,8192]{2,1,0:T(2,128)(2,1)S(1)}, u32[]{:S(2)}, u32[]{:S(2)}) %all-to-all-start) | async-done | bytes 2097184 | tf_op jit(solution)/shard_map/all_to_all | solution.py:96
  194.4 6.7 reshape.230
  201.1 2.5 copy.53
  203.6 0.0 copy-start.7
  203.7 0.0 copy-start.10
  203.7 0.7 convolution_bitcast_fusion.2
  204.4 0.3 copy-done.7
  204.7 0.8 fusion.7
  205.5 0.2 fusion.23
  205.6 0.1 copy-done.8
  205.7 0.7 convolution_bitcast_fusion.1
  206.4 1.9 fusion.20
  208.4 0.0 all-gather.9.cloned.1.call-update
  208.4 0.0 all-gather.7.cloned.1.call-start
  208.5 0.1 convert_reduce_fusion
  208.6 0.1 bitcast_multiply_fusion
  208.6 87.3 %all_gather.17 = f32[64,8,1,128]{3,1,2,0:T(8,128)} all-gather(f32[1,8,1,128]{3,1,2,0:T(8,128)S(1)} %bitcast_multiply_fusion), channel_id=1, replica_groups=mesh['tm'=64,'mp'=8] {'tm'}, dimensions={0}, use_global_device_ids=true | all-gather | bytes 266240 | tf_op jit(solution)/shard_map/all_gather | solution.py:12
  295.9 1.9 fusion
  297.9 0.7 copy-done.1
  298.6 0.6 convolution_select_fusion
  299.2 1.1 fusion.33
  300.3 196.3 %all-gather.9.cloned.1.call-done = f32[512,128,128]{2,1,0:T(8,128)} async-done(((f32[8,128,128]{2,1,0:T(8,128)}), f32[512,128,128]{2,1,0:T(8,128)}) %all-gather.9.cloned.1.call-update) | async-done | bytes 33554448 | tf_op jit(solution)/shard_map/all_gather | solution.py:12
  496.6 0.2 while.12
  496.8 1.8 multiply_reduce_fusion
  498.6 0.1 multiply_multiply_fusion
  498.8 0.6 fusion.2
  499.4 0.2 copy.47
  499.6 2.5 multiply_convert_fusion
  502.1 0.0 all-gather.7.cloned.1.call-update
  502.1 0.0 reduce-scatter.2.cloned.1.call-start
  502.1 147.1 %all-gather.7.cloned.1.call-done = bf16[512,1024]{1,0:T(8,128)(2,1)} async-done(((bf16[512,128]{1,0:T(8,128)(2,1)}), bf16[512,1024]{1,0:T(8,128)(2,1)}) %all-gather.7.cloned.1.call-update) | async-done | bytes 1048592 | tf_op jit(solution)/shard_map/all_gather | solution.py:127
  649.2 2.8 fusion.34
  652.1 0.0 reduce-scatter.2.cloned.1.call-update
  652.1 1.1 convolution_convert_fusion
  653.2 693.9 %reduce-scatter.2.cloned.1.call-done = f32[16,256]{1,0:T(8,128)} async-done(((f32[1024,256]{1,0:T(8,128)}), f32[16,256]{1,0:T(8,128)}) %reduce-scatter.2.cloned.1.call-update) | async-done | bytes 16400 | tf_op jit(solution)/shard_map/reduce_scatter | solution.py:134
  (24 shorter events, 0.2 us)
Async XLA Ops:
  7.2 196.5 %copy-start = (bf16[2048,128]{1,0:T(8,128)(2,1)S(1)}, bf16[2048,128]{1,0:T(8,128)(2,1)}, u32[]{:S(2)}) copy-start(bf16[2048,128]{1,0:T(8,128)(2,1)} %param.18) | copy-start | bytes 1572868
  7.2 39.3 %all-gather.5.cloned.1.call-start = ((), (), s32[]{:S(2)}) async-start(), calls=%async_computation.2 | async-start | bytes 2359296 | tf_op jit(solution)/shard_map/all_gather | solution.py:95
  80.7 15.8 %copy-start.5 = (s32[8,64]{1,0:T(8,128)S(1)}, s32[8,64]{1,0:T(8,128)}, u32[]{:S(2)}) copy-start(s32[8,64]{1,0:T(8,128)} %param.16) | copy-start | bytes 6148
  80.7 113.6 %all-to-all-start = ((bf16[64,2,8192]{2,1,0:T(2,128)(2,1)}), bf16[64,2,8192]{2,1,0:T(2,128)(2,1)S(1)}, u32[]{:S(2)}, u32[]{:S(2)}) async-start(bf16[64,2,8192]{2,1,0:T(2,128)(2,1)} %reshape.229), calls=%async_computation | async-start | bytes 4194304 | tf_op jit(solution)/shard_map/all_to_all | solution.py:96
  96.5 400.1 %all-gather.9.cloned.1.call-start = ((), (), s32[]{:S(2)}) async-start(), calls=%async_computation.5 | async-start | bytes 34078720 | tf_op jit(solution)/shard_map/all_gather | solution.py:12
  203.6 1.0 copy-start.7
  203.7 1.0 copy-start.10
  204.7 1.0 copy-start.8
  205.7 2.7 copy-start.4
  208.4 440.8 %all-gather.7.cloned.1.call-start = ((), (), s32[]{:S(2)}) async-start(), calls=%async_computation.3 | async-start | bytes 1179648 | tf_op jit(solution)/shard_map/all_gather | solution.py:127
  297.8 0.7 copy-start.1
  496.6 2.0 copy-start.6
  499.6 149.7 %copy-start.3 = (bf16[8,64,256]{2,1,0:T(8,128)(2,1)S(1)}, bf16[8,64,256]{2,1,0:T(8,128)(2,1)}, u32[]{:S(2)}) copy-start(bf16[8,64,256]{2,1,0:T(8,128)(2,1)} %param.25) | copy-start | bytes 786436
  502.1 150.0 %copy-start.9 = (bf16[1024,256]{1,0:T(8,128)(2,1)S(1)}, bf16[1024,256]{1,0:T(8,128)(2,1)}, u32[]{:S(2)}) copy-start(bf16[1024,256]{1,0:T(8,128)(2,1)} %param.24) | copy-start | bytes 1572868
  502.1 845.1 %reduce-scatter.2.cloned.1.call-start = ((), (), s32[]{:S(2)}) async-start(), calls=%async_computation.4 | async-start | bytes 1064960 | tf_op jit(solution)/shard_map/reduce_scatter | solution.py:134
  649.2 2.9 copy-start.2
Sparse Core Ops, SparseCore 0:
  10.2 36.2 all-gather.4
  208.5 287.9 all-gather.8
  502.2 146.9 all-gather.6
  654.0 693.0 reduce-scatter.1
where the time goes:
time: 1360 us; the launch traced here: 1350 us
  waiting for transfers between devices  1170 us (86%)
  blocking collectives  87.3 us (6%)
  local copies, waits for them, and re-layouts  23.5 us (2%)
  other arithmetic  22.3 us (2%)
  matrix products  16.5 us (1%)
  starting transfers between devices  15.9 us (1%)
  between operations  14 us (1%)
    reduce_scatter x1, waiting for transfers between devices, local(): lax.psum_scatter(partial_grad, 'tm', scatter_dimension=0, tiled=True)  694 us
    all_gather x1, waiting for transfers between devices, prefix(): gathered = jax.tree.map(lambda a: lax.all_gather(a, axis), part)  196 us
    all_gather x1, waiting for transfers between devices, local(): portion = lax.all_gather(gated_rows, 'mp', axis=1, tiled=True)  147 us
    all_to_all x1, waiting for transfers between devices, local(): lax.all_to_all(full_rows, 'tm', split_axis=1, concat_axis=0, tiled=True)  97.4 us
    all_gather x1, blocking collectives, prefix(): gathered = jax.tree.map(lambda a: lax.all_gather(a, axis), part)  87.3 us
    all_gather x1, waiting for transfers between devices, local(): full_rows = lax.all_gather(observations, 'mp', axis=2, tiled=True)  38.6 us
  transfers between devices with their start and end apart: 5, of which 5 were waited for; matrix products, arithmetic and copies ran while one was open for 0% of the time, Pallas kernels for 0%

commit v1 on v0

--- a/solution.py
+++ b/solution.py
@@ -5,6 +5,16 @@
 
 HK = 128
 CH = 8
+
+
+def pass_along(shard, name, dim):
+    count = lax.axis_size(name)
+    moving, blocks = (shard, [shard])
+    for _ in range(count - 1):
+        moving = lax.ppermute(moving, name, [(i, (i + 1) % count) for i in range(count)])
+        blocks.insert(0, moving)
+    line = jnp.concatenate(blocks, axis=dim)
+    return jnp.roll(line, (lax.axis_index(name) + 1) * shard.shape[dim], axis=dim)
 
 
 def prefix(part, axis, combine, identity):
@@ -124,7 +134,7 @@
     gated = finish(attended, projected[4], norm_gain, contact)
     gated_rows = gated.reshape(characters * frames, -1)
     cotangent_rows = out_cotangent.reshape(characters * frames, -1)
-    portion = lax.all_gather(gated_rows, "mp", axis=1, tiled=True)
+    portion = pass_along(gated_rows, "mp", 1)
     produced = jnp.dot(portion, out_weight, preferred_element_type=jnp.float32)
     gradient_piece = lax.dot_general(
         portion, cotangent_rows, (((0,), (0,)), ((), ())), preferred_element_type=jnp.float32

time: 1360 us -> 1360 us (level)
    all_gather x1 -> x0, waiting for transfers between devices: 147 us -> none  [local(): portion = lax.all_gather(gated_rows, 'mp', axis=1, tiled=True)]
    reduce_scatter x1, waiting for transfers between devices: 694 us -> 812 us  [local(): lax.psum_scatter(partial_grad, 'tm', scatter_dimension=0, tiled=True)]
    ppermute x0 -> x7, waiting for transfers between devices: none -> 32.2 us  [pass_along(): lax.ppermute(moving, name, [(i, (i + 1) % count) for i in range(count)])]
  transfers between devices with their start and end apart: 5 -> 11, of which waited for: 5 -> 11; matrix products, arithmetic and copies ran while one was open for 0% -> 0% of each run, Pallas kernels for 0% -> 0%
where the time goes in v1:
time: 1360 us
  waiting for transfers between devices  1180 us (87%)
  blocking collectives  87 us (6%)
  local copies, waits for them, and re-layouts  25.9 us (2%)
  other arithmetic  22.3 us (2%)
  starting transfers between devices  15.9 us (1%)
  matrix products  14.5 us (1%)
  between operations  14.1 us (1%)
    reduce_scatter x1, waiting for transfers between devices, local(): lax.psum_scatter(partial_grad, 'tm', scatter_dimension=0, tiled=True)  812 us
    all_gather x1, waiting for transfers between devices, prefix(): gathered = jax.tree.map(lambda a: lax.all_gather(a, axis), part)  197 us
    all_to_all x1, waiting for transfers between devices, local(): lax.all_to_all(full_rows, 'tm', split_axis=1, concat_axis=0, tiled=True)  97.4 us
    all_gather x1, blocking collectives, prefix(): gathered = jax.tree.map(lambda a: lax.all_gather(a, axis), part)  87 us
    all_gather x1, waiting for transfers between devices, local(): full_rows = lax.all_gather(observations, 'mp', axis=2, tiled=True)  38.6 us
    ppermute x7, waiting for transfers between devices, pass_along(): lax.ppermute(moving, name, [(i, (i + 1) % count) for i in range(count)])  32.2 us
  transfers between devices with their start and end apart: 11, of which 11 were waited for; matrix products, arithmetic and copies ran while one was open for 0% of the time, Pallas kernels for 0%

profile of v1, /device:TPU:8, one launch (start us, length us, event | category | flops | bytes accessed | tf_op | source)
XLA Modules:
  0.0 1357.8 jit_solution(1351628585651975578)
XLA Ops:
  7.2 0.7 all-gather.4.cloned.1.call-update
  7.9 38.6 %all-gather.4.cloned.1.call-done = bf16[1,4096,256]{1,2,0:T(8,128)(2,1)} async-done(((bf16[1,4096,32]{1,2,0:T(8,128)(2,1)}), bf16[1,4096,256]{1,2,0:T(8,128)(2,1)}) %all-gather.4.cloned.1.call-update) | async-done | bytes 2097168 | tf_op jit(solution)/shard_map/all_gather | solution.py:105
  46.5 10.0 copy.41
  56.5 0.5 broadcast.80
  57.0 21.6 %reduce.4 = bf16[4096,256]{1,0:T(8,128)(2,1)S(1)} reduce(bf16[4096,1,256]{2,1,0:T(2,128)(2,1)} %bitcast.125, bf16[]{:T(256)} %broadcast.80), dimensions={1}, to_apply=%bitcast.99.reduce_sub_computation | reduce | bytes 4194306
  78.6 2.0 reshape.229
  80.6 15.7 %all-to-all-start = ((bf16[64,2,8192]{2,1,0:T(2,128)(2,1)}), bf16[64,2,8192]{2,1,0:T(2,128)(2,1)S(1)}, u32[]{:S(2)}, u32[]{:S(2)}) async-start(bf16[64,2,8192]{2,1,0:T(2,128)(2,1)} %reshape.229), calls=%async_computation | async-start | bytes 4194304 | tf_op jit(solution)/shard_map/all_to_all | solution.py:106
  96.4 0.0 all-gather.6.cloned.1.call-start
  96.5 0.2 reduce_window_sum.24
  96.7 0.2 slice_reduce_fusion
  96.9 0.1 compare_convert_fusion.1
  96.9 97.4 %all-to-all-done = bf16[64,2,8192]{2,1,0:T(2,128)(2,1)S(1)} async-done(((bf16[64,2,8192]{2,1,0:T(2,128)(2,1)}), bf16[64,2,8192]{2,1,0:T(2,128)(2,1)S(1)}, u32[]{:S(2)}, u32[]{:S(2)}) %all-to-all-start) | async-done | bytes 2097184 | tf_op jit(solution)/shard_map/all_to_all | solution.py:106
  194.3 6.7 reshape.230
  201.0 2.5 copy.53
  203.6 0.7 convolution_bitcast_fusion.2
  204.3 0.3 copy-done.6
  204.6 0.8 fusion.10
  205.4 0.2 fusion.26
  205.6 0.1 copy-done.7
  205.7 0.7 convolution_bitcast_fusion.1
  206.4 1.9 fusion.23
  208.3 0.0 reduce-scatter.2.cloned.1.call-start
  208.4 0.1 convert_reduce_fusion
  208.5 0.1 bitcast_multiply_fusion
  208.6 87.0 %all_gather.14 = f32[64,8,1,128]{3,1,2,0:T(8,128)} all-gather(f32[1,8,1,128]{3,1,2,0:T(8,128)S(1)} %bitcast_multiply_fusion), channel_id=1, replica_groups=mesh['tm'=64,'mp'=8] {'tm'}, dimensions={0}, use_global_device_ids=true | all-gather | bytes 266240 | tf_op jit(solution)/shard_map/all_gather | solution.py:22
  295.6 1.9 fusion
  297.5 0.7 copy-done.1
  298.2 0.6 convolution_select_fusion
  298.8 1.1 fusion.38
  299.9 196.8 %all-gather.6.cloned.1.call-done = f32[512,128,128]{2,1,0:T(8,128)} async-done(((f32[8,128,128]{2,1,0:T(8,128)}), f32[512,128,128]{2,1,0:T(8,128)}) %all-gather.6.cloned.1.call-update) | async-done | bytes 33554448 | tf_op jit(solution)/shard_map/all_gather | solution.py:22
  496.7 0.2 while.12
  496.9 1.8 multiply_reduce_fusion
  498.7 0.1 multiply_multiply_fusion
  498.9 0.6 fusion.2
  499.5 0.2 copy.47
  499.8 1.8 multiply_convert_fusion
  501.5 4.4 collective-permute-done
  505.9 4.4 collective-permute-done.1
  510.3 4.4 collective-permute-done.2
  514.7 4.4 collective-permute-done.3
  519.1 4.4 collective-permute-done.4
  523.5 4.6 collective-permute-done.5
  528.1 5.7 collective-permute-done.6
  533.8 0.9 constant_dynamic-update-slice_fusion.15
  535.1 0.9 constant_dynamic-update-slice_fusion.7
  536.4 1.5 fusion.5
  537.9 1.2 convolution_convert_fusion
  539.0 812.2 %reduce-scatter.2.cloned.1.call-done = f32[16,256]{1,0:T(8,128)} async-done(((f32[1024,256]{1,0:T(8,128)}), f32[16,256]{1,0:T(8,128)}) %reduce-scatter.2.cloned.1.call-update) | async-done | bytes 16400 | tf_op jit(solution)/shard_map/reduce_scatter | solution.py:144
  (49 shorter events, 0.9 us)
Async XLA Ops:
  7.2 196.4 %copy-start = (bf16[2048,128]{1,0:T(8,128)(2,1)S(1)}, bf16[2048,128]{1,0:T(8,128)(2,1)}, u32[]{:S(2)}) copy-start(bf16[2048,128]{1,0:T(8,128)(2,1)} %param.18) | copy-start | bytes 1572868
  7.2 39.3 %all-gather.4.cloned.1.call-start = ((), (), s32[]{:S(2)}) async-start(), calls=%async_computation.2 | async-start | bytes 2359296 | tf_op jit(solution)/shard_map/all_gather | solution.py:105
  80.6 15.8 %copy-start.4 = (s32[8,64]{1,0:T(8,128)S(1)}, s32[8,64]{1,0:T(8,128)}, u32[]{:S(2)}) copy-start(s32[8,64]{1,0:T(8,128)} %param.16) | copy-start | bytes 6148
  80.6 113.6 %all-to-all-start = ((bf16[64,2,8192]{2,1,0:T(2,128)(2,1)}), bf16[64,2,8192]{2,1,0:T(2,128)(2,1)S(1)}, u32[]{:S(2)}, u32[]{:S(2)}) async-start(bf16[64,2,8192]{2,1,0:T(2,128)(2,1)} %reshape.229), calls=%async_computation | async-start | bytes 4194304 | tf_op jit(solution)/shard_map/all_to_all | solution.py:106
  96.4 400.3 %all-gather.6.cloned.1.call-start = ((), (), s32[]{:S(2)}) async-start(), calls=%async_computation.4 | async-start | bytes 34078720 | tf_op jit(solution)/shard_map/all_gather | solution.py:22
  203.6 1.0 copy-start.6
  203.6 1.0 copy-start.9
  204.6 1.0 copy-start.7
  205.7 2.7 copy-start.3
  208.3 1142.9 %reduce-scatter.2.cloned.1.call-start = ((), (), s32[]{:S(2)}) async-start(), calls=%async_computation.3 | async-start | bytes 1064960 | tf_op jit(solution)/shard_map/reduce_scatter | solution.py:144
  297.5 0.7 copy-start.1
  496.7 2.0 copy-start.5
  501.5 4.4 collective-permute-start
  505.9 4.4 collective-permute-start.1
  510.3 4.4 collective-permute-start.2
  514.7 4.4 collective-permute-start.3
  519.1 4.4 collective-permute-start.4
  523.5 4.6 collective-permute-start.5
  528.1 5.7 collective-permute-start.6
  528.1 8.3 copy-start.2
  536.2 1.6 copy-start.8
Sparse Core Ops, SparseCore 0:
  10.2 36.2 all-gather.3
  208.5 288.1 all-gather.5
  538.0 813.2 reduce-scatter.1
